TPU v7x, 32 devices: a whole 2x2x4 slice. The times are simulated.
32 devices in a mesh: grp: 4 (over y, x), sp: 8 (over z, core).
Axes of the slice: x: 2, y: 2, z: 4, core: 2. Of those that a mesh axis runs over, the one named last changes fastest.
Arguments:
- coarse: bfloat16 [64, 48, 1024], P(('grp', 'sp')), parts along dimension 0, may hold values from -30 to 30
- conv_weight: bfloat16 [1024, 3, 3, 1024], P('sp'), may hold values from -0.104166667 to 0.104166667
- conv_bias: float32 [1024], P('sp'), may hold values from -5 to 5
- norm_gain: float32 [1024], P('sp'), may hold values from 0.5 to 1.5
- norm_shift: float32 [1024], P('sp'), may hold values from -3 to 3
- up_weight: bfloat16 [512, 2, 2, 1024], P('sp'), may hold values from -0.1875 to 0.1875
- up_bias: bfloat16 [512], P('sp'), may hold values from -3 to 3
Outputs:
- fine: bfloat16 [128, 96, 512], P(('grp', 'sp')), parts along dimension 0
There are 4 independent parts, one for each index of `grp`. A program takes and returns all parts, laid end to end along the dimension named above; an argument that names none is the same for every part. Nothing has to cross between parts.
All inputs are finite; a program needn't handle non-finite values.
Results may differ from a plain program's by a relative error of at most 0.0042.
Values may be sent and summed in bfloat16 or wider, within the bound.
A program may use at most 64 MiB of HBM per device.

v0:
```python
import jax
import jax.numpy as jnp
from jax import lax
from jax.sharding import PartitionSpec as P

GSIZE = 32


def conv_rows(weights_cat, width_cols, channels, outputs, tile_rows):
    how_many = tile_rows.shape[0]
    padded = jnp.pad(tile_rows, ((0, 0), (1, 1), (0, 0)))
    partial_sum = jnp.zeros((how_many * width_cols, 3 * outputs), jnp.float32)
    for offset in range(3):
        window = padded[:, offset : offset + width_cols, :].reshape(how_many * width_cols, channels)
        partial_sum = partial_sum + jnp.dot(
            window, weights_cat[offset], preferred_element_type=jnp.float32
        )
    partial_sum = partial_sum.reshape(how_many, width_cols, 3, outputs)
    contrib = jnp.zeros((how_many + 2, width_cols, outputs), jnp.float32)
    for kernel_row in range(3):
        contrib = contrib.at[2 - kernel_row : 2 - kernel_row + how_many].add(
            partial_sum[:, :, kernel_row]
        )
    return contrib


def normalize(convolved, height, width_cols, outputs, norm_gain, norm_shift):
    grouped = convolved.reshape(height, width_cols, outputs // GSIZE, GSIZE)
    centre = jnp.mean(grouped, axis=(0, 1, 3), keepdims=True)
    spread = jnp.mean(jnp.square(grouped - centre), axis=(0, 1, 3), keepdims=True)
    normed = ((grouped - centre) * lax.rsqrt(spread + 1e-05)).reshape(height, width_cols, outputs)
    return jax.nn.silu(normed * norm_gain + norm_shift).astype(jnp.bfloat16)


def full_conv(coarse, conv_weight, conv_bias, norm_gain, norm_shift):
    tile_count = lax.axis_size("sp")
    local_rows, width_cols, channels = coarse.shape
    height = local_rows * tile_count
    outputs = conv_weight.shape[0]
    weights_cat = jnp.transpose(conv_weight, (2, 3, 1, 0)).reshape(3, channels, 3 * outputs)
    summed = conv_rows(
        weights_cat, width_cols, channels, outputs, lax.all_gather(coarse, "sp", axis=0, tiled=True)
    )
    convolved = summed[1 : height + 1] + conv_bias
    return normalize(convolved, height, width_cols, outputs, norm_gain, norm_shift)


def body(coarse, conv_weight, conv_bias, norm_gain, norm_shift, up_weight, up_bias):
    activated = full_conv(coarse, conv_weight, conv_bias, norm_gain, norm_shift)
    height, width_cols, channels = (activated.shape[0], activated.shape[1], conv_weight.shape[3])
    slice_out = up_weight.shape[0]
    flat_weight = jnp.transpose(up_weight, (3, 1, 2, 0)).reshape(channels, 4 * slice_out)
    features = lax.all_gather(activated, "sp", axis=2, tiled=True)
    chosen_width = features.shape[2]
    flat_features = features.reshape(height * width_cols, chosen_width)
    decoded = jnp.dot(flat_features, flat_weight, preferred_element_type=jnp.float32)
    decoded = (decoded.reshape(height, width_cols, 2, 2, slice_out) + up_bias).astype(jnp.bfloat16)
    decoded = jnp.transpose(decoded, (0, 2, 1, 3, 4)).reshape(2 * height, 2 * width_cols, slice_out)
    return lax.all_to_all(decoded, "sp", split_axis=0, concat_axis=2, tiled=True)


def solution(mesh):
    return jax.shard_map(
        body,
        mesh=mesh,
        in_specs=(
            P(("grp", "sp"), None, None),
            P("sp", None, None, None),
            P("sp"),
            P("sp"),
            P("sp"),
            P("sp", None, None, None),
            P("sp"),
        ),
        out_specs=P(("grp", "sp"), None, None),
        check_vma=False,
    )
```

profile of v0, /device:TPU:1, one launch (start us, length us, event | category | flops | bytes accessed | tf_op | source)
XLA Modules:
  0.0 104.7 jit_solution(12702812337742161823)
XLA Ops:
  6.5 0.7 all-gather.3.cloned.1.call-update
  7.3 1.9 %fusion.11 = (bf16[1,1024,3,128]{1,3,0,2:T(8,128)(2,1)S(1)}, bf16[1,1024,3,128]{1,3,0,2:T(8,128)(2,1)S(1)}, bf16[1,1024,3,128]{1,3,0,2:T(8,128)(2,1)S(1)}) fusion(bf16[3,1024,3,128]{1,3,0,2:T(8,128)(2,1)} %bitcast.54), kind=kLoop, calls=%fused_computation.19 | loop fusion | bytes 4718592 | tf_op jit(solution)/shard_map/slice | solution.py:16
  9.2 27.3 %all-gather.3.cloned.1.call-done = bf16[16,48,1024]{2,1,0:T(8,128)(2,1)} async-done(((bf16[2,48,1024]{2,1,0:T(8,128)(2,1)}), bf16[16,48,1024]{2,1,0:T(8,128)(2,1)}) %all-gather.3.cloned.1.call-update) | async-done | bytes 1572880 | tf_op jit(solution)/shard_map/all_gather | solution.py:42
  36.6 3.5 %pad_slice_fusion = (bf16[16,48,1024]{2,1,0:T(8,128)(2,1)S(1)}, bf16[16,48,1024]{2,1,0:T(8,128)(2,1)S(1)}) fusion(bf16[16,48,1024]{2,1,0:T(8,128)(2,1)} %all-gather.3.cloned.1.call-done), kind=kLoop, calls=%fused_computation | loop fusion | bytes 4718592 | tf_op jit(solution)/shard_map/slice | solution.py:14
  40.1 1.0 fusion.13
  41.1 0.4 copy-done
  41.5 1.0 convolution_add_fusion.1
  42.5 1.0 convolution_add_fusion
  43.5 0.5 reshape.148
  44.1 0.8 fusion.12
  45.2 0.4 copy-done.1
  45.6 0.1 fusion.10
  45.8 0.1 reduce_sum.25
  46.0 0.1 sub.19
  46.0 0.1 multiply_reduce_fusion
  46.3 0.1 reduce_sum.37
  46.5 0.1 mul.26
  46.5 0.8 multiply_convert_fusion
  47.4 26.8 %all-gather.5.cloned.1.call-done = bf16[16,48,1024]{2,1,0:T(8,128)(2,1)} async-done(((bf16[16,48,128]{2,1,0:T(8,128)(2,1)}), bf16[16,48,1024]{2,1,0:T(8,128)(2,1)}) %all-gather.5.cloned.1.call-update) | async-done | bytes 1572880 | tf_op jit(solution)/shard_map/all_gather | solution.py:53
  74.3 2.4 %fusion.4 = bf16[16,2,48,2,64]{4,2,3,1,0:T(8,128)(2,1)S(1)} fusion(bf16[16,48,1024]{2,1,0:T(8,128)(2,1)} %all-gather.5.cloned.1.call-done, f32[64]{0:T(128)S(1)} %convert_element_type.16, bf16[64,2,2,1024]{3,2,1,0:T(2,128)(2,1)S(1)} %copy-done.4), kind=kOutput, calls=%fused_computation.7 | convolution fusion | flops 403046400 | bytes 2490624 | tf_op jit(solution)/shard_map/dot_general | solution.py:56
  76.7 0.8 copy.23
  77.5 0.3 copy.24
  77.8 19.0 %all_to_all.18 = bf16[32,96,64]{1,2,0:T(8,128)(2,1)S(1)} all-to-all(bf16[32,96,64]{1,2,0:T(8,128)(2,1)S(1)} %copy.24), channel_id=1, replica_groups=mesh['grp'=4,'sp'=8] {'sp'}, dimensions={0} | all-to-all | bytes 786432 | tf_op jit(solution)/shard_map/all_to_all | solution.py:59
  96.9 1.0 copy.26
  (24 shorter events, 0.7 us)
Async XLA Ops:
  6.5 30.0 %all-gather.3.cloned.1.call-start = ((), (), s32[]{:S(2)}) async-start(), calls=%async_computation.1 | async-start | bytes 1769472 | tf_op jit(solution)/shard_map/all_gather | solution.py:42
  7.3 67.0 %all-gather.5.cloned.1.call-start = ((), (), s32[]{:S(2)}) async-start(), calls=%async_computation.2 | async-start | bytes 1769472 | tf_op jit(solution)/shard_map/all_gather | solution.py:53
  40.1 1.4 %copy-start = (bf16[16,48,1024]{2,1,0:T(8,128)(2,1)S(1)}, bf16[16,48,1024]{2,1,0:T(8,128)(2,1)}, u32[]{:S(2)}) copy-start(bf16[16,48,1024]{2,1,0:T(8,128)(2,1)} %all-gather.3.cloned.1.call-done) | copy-start | bytes 4718596
  44.9 0.7 copy-start.1
  44.9 1.6 %copy-start.2 = (f32[128]{0:T(128)S(1)}, f32[128]{0:T(128)}, u32[]{:S(2)}) copy-start(f32[128]{0:T(128)} %param.17) | copy-start | bytes 1540
  45.0 1.6 %copy-start.3 = (f32[128]{0:T(128)S(1)}, f32[128]{0:T(128)}, u32[]{:S(2)}) copy-start(f32[128]{0:T(128)} %param.16) | copy-start | bytes 1540
  45.1 2.4 %copy-start.5 = (bf16[64]{0:T(256)(128)(2,1)S(1)}, bf16[64]{0:T(256)(128)(2,1)}, u32[]{:S(2)}) copy-start(bf16[64]{0:T(256)(128)(2,1)} %param.19) | copy-start | bytes 388
  45.1 29.2 %copy-start.4 = (bf16[64,2,2,1024]{3,2,1,0:T(2,128)(2,1)S(1)}, bf16[64,2,2,1024]{3,2,1,0:T(2,128)(2,1)}, u32[]{:S(2)}) copy-start(bf16[64,2,2,1024]{3,2,1,0:T(2,128)(2,1)} %param.18) | copy-start | bytes 1572868
Sparse Core Ops, SparseCore 0:
  9.0 27.5 all-gather.2
  47.5 26.7 all-gather.4
where the time goes:
time: 106 us; the launch traced here: 105 us
  waiting for transfers between devices  54.9 us (52%)
  blocking collectives  19 us (18%)
  between operations  13.6 us (13%)
  local copies, waits for them, and re-layouts  10.2 us (10%)
  matrix products  5.45 us (5%)
  other arithmetic  1.51 us (1%)
    all_gather x1, waiting for transfers between devices, full_conv(): lax.all_gather(coarse, 'sp', axis=0, tiled=True)  27.3 us
    all_gather x1, waiting for transfers between devices, body(): features = lax.all_gather(activated, 'sp', axis=2, tiled=True)  26.8 us
    all_to_all x1, blocking collectives, body(): lax.all_to_all(decoded, 'sp', split_axis=0, concat_axis=2, tiled=True)  19 us
    slice x1, local copies, waits for them, and re-layouts, conv_rows(): padded[:, offset:offset + width_cols, :]  3.53 us
    dot_general x3, matrix products, conv_rows(): jnp.dot(window, weights_cat[offset], preferred_element_type=jnp.float32)  3.02 us
    dot_general x1, matrix products, body(): jnp.dot(flat_features, flat_weight, preferred_element_type=jnp.float32)  2.43 us
  transfers between devices with their start and end apart: 2, of which 2 were waited for; matrix products, arithmetic and copies ran while one was open for 2% of the time, Pallas kernels for 0%

commit v1 on v0

v1 whole, which is shorter than its diff:
```python
import functools

import jax
import jax.numpy as jnp
from jax import lax
from jax.experimental import pallas as pl
from jax.experimental.pallas import tpu as pltpu
from jax.sharding import PartitionSpec as P

GSIZE = 32
TAPS = 4
NT = (((1,), (1,)), ((), ()))


def kernel(
    chips,
    coarse,
    conv_w,
    up_w,
    conv_bias,
    gain,
    shift,
    up_bias,
    out,
    gathered,
    w_vmem,
    up_all,
    summed,
    act,
    act_all,
    bias_own,
    bias_all,
    local_sem,
    c_line,
    c_sib,
    c_recv,
    u_line,
    u_xy,
    u_sib,
    u_recv,
    b_send,
    b_recv,
    a_send,
    a_recv,
):
    devices = 2 * chips
    rows, width, channels = coarse.shape
    outputs = conv_w.shape[0] // 9
    slice_out = up_w.shape[1]
    decoded = devices * slice_out
    me = lax.axis_index("sp")
    col = lax.axis_index("grp")
    z = me // 2
    core = me % 2
    sibling = 2 * z + 1 - core
    part = col % TAPS
    base = col - part

    def at(column, index):
        return {"grp": column, "sp": index}

    def remote(src, dst, send, recv, device):
        return pltpu.make_async_remote_copy(
            src_ref=src,
            dst_ref=dst,
            send_sem=send,
            recv_sem=recv,
            device_id=device,
            device_id_type=pl.DeviceIdType.MESH,
        )

    def onward(direction):
        return (z + 1, z + 1 < chips) if direction == 0 else (z - 1, z - 1 >= 0)

    def origin(direction, k):
        return (z - k, z - k >= 0) if direction == 0 else (z + k, z + k < chips)

    def coarse_line(direction, src, h, ref):
        b = 2 * src + core
        target = 2 * onward(direction)[0] + core
        return remote(ref, gathered.at[b, h], c_line.at[direction, src, h], c_recv.at[b, h], at(col, target))

    def coarse_sib(src, h, ref):
        b = 2 * src + core
        return remote(ref, gathered.at[b, h], c_sib.at[src, h], c_recv.at[b, h], at(col, sibling))

    def coarse_wait(b, h):
        remote(gathered.at[b, h], gathered.at[b, h], c_sib.at[0, h], c_recv.at[b, h], at(col, sibling)).wait_recv()

    def up_line(direction, src, ref):
        b = 2 * src + core
        target = 2 * onward(direction)[0] + core
        return remote(ref, up_all.at[part, b], u_line.at[direction, src], u_recv.at[b, part], at(col, target))

    def up_xy(q, src):
        b = 2 * src + core
        ref = up_all.at[part, b]
        return remote(ref, ref, u_xy.at[q - 1, src], u_recv.at[b, part], at(base + (part + q) % TAPS, me))

    def up_sib(src, tap, ref):
        b = 2 * src + core
        return remote(ref, up_all.at[tap, b], u_sib.at[src, tap], u_recv.at[b, tap], at(col, sibling))

    def up_wait(b, tap):
        ref = up_all.at[tap, b]
        remote(ref, ref, u_sib.at[0, tap], u_recv.at[b, tap], at(col, sibling)).wait_recv()

    w_copy = pltpu.make_async_copy(conv_w, w_vmem, local_sem.at[0])
    own_copy = pltpu.make_async_copy(coarse, gathered.at[me], local_sem.at[1])
    up_copies = [
        pltpu.make_async_copy(up_w.at[tap], up_all.at[tap, me], local_sem.at[2 + tap]) for tap in range(TAPS)
    ]
    w_copy.start()
    own_copy.start()
    for copy in up_copies:
        copy.start()

    barrier = pltpu.get_barrier_semaphore()

    def greet(i, carry):
        other = lax.rem(me + i, devices)
        pl.semaphore_signal(barrier, inc=1, device_id=at(col, other), device_id_type=pl.DeviceIdType.MESH)
        return carry

    lax.fori_loop(1, devices, greet, 0)
    for q in range(1, TAPS):
        pl.semaphore_signal(
            barrier, inc=1, device_id=at(base + (part + q) % TAPS, me), device_id_type=pl.DeviceIdType.MESH
        )
    pl.semaphore_wait(barrier, devices - 1 + TAPS - 1)

    for h in range(rows):
        for direction in range(2):

            @pl.when(onward(direction)[1])
            def _():
                coarse_line(direction, z, h, coarse.at[h]).start()

        coarse_sib(z, h, coarse.at[h]).start()
    for direction in range(2):

        @pl.when(onward(direction)[1])
        def _():
            up_line(direction, z, up_w.at[part]).start()

    for tap in range(TAPS):
        up_sib(z, tap, up_w.at[tap]).start()

    lanes = lax.broadcasted_iota(jnp.int32, (slice_out, decoded), 1)
    line = lax.broadcasted_iota(jnp.int32, (slice_out, decoded), 0)
    chosen = (lanes == line + me * slice_out).astype(jnp.float32)
    placed = jnp.dot(up_bias[...], chosen, preferred_element_type=jnp.float32, precision=lax.Precision.HIGHEST)
    bias_own[...] = placed
    bias_all[me] = placed

    def bias_copy(other, slot):
        return remote(bias_own, bias_all.at[slot], b_send.at[other], b_recv.at[slot], at(col, other))

    def send_bias(i, carry):
        bias_copy(lax.rem(me + i, devices), me).start()
        return carry

    lax.fori_loop(1, devices, send_bias, 0)

    summed[...] = jnp.zeros_like(summed)
    count = 2 * rows * width
    column = lax.broadcasted_iota(jnp.int32, (count, outputs), 0) % width

    def conv_pair(src):
        block = gathered[pl.ds(2 * src, 2)].reshape(count, channels)
        if outputs % 128 == 0:
            product = lax.dot_general(block, w_vmem[...], NT, preferred_element_type=jnp.float32)
            taps = [product[:, t * outputs : (t + 1) * outputs] for t in range(9)]
        else:
            taps = [
                lax.dot_general(
                    block, w_vmem[t * outputs : (t + 1) * outputs], NT, preferred_element_type=jnp.float32
                )
                for t in range(9)
            ]
        for r in range(3):
            left, middle, right = taps[3 * r : 3 * r + 3]
            total = (
                middle
                + jnp.where(column == 0, 0.0, pltpu.roll(left, 1, 0))
                + jnp.where(column == width - 1, 0.0, pltpu.roll(right, count - 1, 0))
            )
            where = pl.ds(2 * rows * src + 2 - r, 2 * rows)
            summed[where] = summed[where] + total.reshape(2 * rows, width, outputs)

    w_copy.wait()
    own_copy.wait()
    for h in range(rows):
        coarse_wait(sibling, h)
    conv_pair(z)

    def spread(k):
        for direction in range(2):
            src, there = origin(direction, k)

            @pl.when(there)
            def _():
                for q in range(1, TAPS):
                    tap = (part + q) % TAPS
                    up_wait(2 * src + core, tap)
                    up_sib(src, tap, up_all.at[tap, 2 * src + core]).start()

    def step(k, carry):
        for direction in range(2):
            src, there = origin(direction, k)

            @pl.when(there)
            def _():
                b = 2 * src + core
                for h in range(rows):
                    coarse_wait(b, h)

                    @pl.when(onward(direction)[1])
                    def _():
                        coarse_line(direction, src, h, gathered.at[b, h]).start()

                    coarse_sib(src, h, gathered.at[b, h]).start()

        for direction in range(2):
            src, there = origin(direction, k)

            @pl.when(there)
            def _():
                b = 2 * src + core
                up_wait(b, part)

                @pl.when(onward(direction)[1])
                def _():
                    up_line(direction, src, up_all.at[part, b]).start()

                for q in range(1, TAPS):
                    up_xy(q, src).start()
                up_sib(src, part, up_all.at[part, b]).start()

        for direction in range(2):
            src, there = origin(direction, k)

            @pl.when(there)
            def _():
                for h in range(rows):
                    coarse_wait(2 * src + 1 - core, h)
                conv_pair(src)

        @pl.when(k > 1)
        def _():
            spread(k - 1)

        return carry

    lax.fori_loop(1, chips, step, 0)

    height = devices * rows
    values = summed[1 : height + 1].reshape(height * width, outputs) + conv_bias[...]
    scale = 1.0 / (height * width * GSIZE)
    same = (
        lax.broadcasted_iota(jnp.int32, (outputs, outputs), 0) // GSIZE
        == lax.broadcasted_iota(jnp.int32, (outputs, outputs), 1) // GSIZE
    ).astype(jnp.float32)

    def group_mean(array):
        each = jnp.broadcast_to(jnp.sum(array, axis=0, keepdims=True), (8, outputs))
        whole = jnp.dot(each, same, preferred_element_type=jnp.float32, precision=lax.Precision.HIGHEST)
        return whole[:1] * scale

    values = values - group_mean(values)
    factor = lax.rsqrt(group_mean(values * values) + 1e-05) * gain[...]
    normed = values * factor + shift[...]
    act[...] = (normed / (1.0 + jnp.exp(-normed))).astype(jnp.bfloat16).reshape(devices, rows * width, outputs)

    def act_copy(other, slot):
        return remote(act.at[other], act_all.at[slot], a_send.at[other], a_recv.at[slot], at(col, other))

    def send_act(i, carry):
        act_copy(lax.rem(me + i, devices), me).start()
        return carry

    lax.fori_loop(1, devices, send_act, 0)
    act_all[me] = act[me]

    spread(chips - 1)

    def arrivals(i, carry):
        other = lax.rem(me + i, devices)
        bias_copy(other, other).wait_recv()
        act_copy(other, other).wait_recv()
        return carry

    lax.fori_loop(1, devices, arrivals, 0)

    def up_arrivals(src, carry):
        for tap in range(TAPS):
            up_wait(2 * src + 1 - core, tap)
        return carry

    lax.fori_loop(0, chips, up_arrivals, 0)
    for copy in up_copies:
        copy.wait()

    bias = jnp.sum(bias_all[...], axis=0)[:1]
    for tap in range(TAPS):
        weight = up_all[tap].reshape(decoded, channels)
        if outputs % 128 == 0:
            features = jnp.concatenate([act_all[s] for s in range(devices)], axis=1)
            fine = lax.dot_general(features, weight, NT, preferred_element_type=jnp.float32)
        else:
            fine = jnp.zeros((rows * width, decoded), jnp.float32)
            for s in range(devices):
                fine = fine + lax.dot_general(
                    act_all[s],
                    weight[:, s * outputs : (s + 1) * outputs],
                    NT,
                    preferred_element_type=jnp.float32,
                )
        a, b = tap // 2, tap % 2
        out[:, a, :, b * decoded : (b + 1) * decoded] = (
            (fine + bias).astype(jnp.bfloat16).reshape(rows, width, decoded)
        )

    def sent(src, carry):
        for h in range(rows):
            coarse_sib(src, h, gathered.at[0, h]).wait_send()
        for tap in range(TAPS):
            up_sib(src, tap, up_all.at[tap, 0]).wait_send()

        @pl.when(src != z)
        def _():
            for q in range(1, TAPS):
                up_xy(q, src).wait_send()

        for direction in range(2):
            passed = src <= z if direction == 0 else src >= z

            @pl.when(jnp.logical_and(passed, onward(direction)[1]))
            def _():
                for h in range(rows):
                    coarse_line(direction, src, h, gathered.at[0, h]).wait_send()
                up_line(direction, src, up_all.at[0, 0]).wait_send()

        return carry

    lax.fori_loop(0, chips, sent, 0)

    def small_sent(i, carry):
        other = lax.rem(me + i, devices)
        bias_copy(other, other).wait_send()
        act_copy(other, other).wait_send()
        return carry

    lax.fori_loop(1, devices, small_sent, 0)


def body(chips, coarse, conv_weight, conv_bias, norm_gain, norm_shift, up_weight, up_bias):
    devices = 2 * chips
    rows, width, channels = coarse.shape
    outputs = conv_weight.shape[0]
    slice_out = up_weight.shape[0]
    decoded = devices * slice_out
    conv_w = jnp.transpose(conv_weight, (1, 2, 0, 3)).reshape(9 * outputs, channels)
    up_w = jnp.transpose(up_weight, (1, 2, 0, 3)).reshape(TAPS, slice_out, channels)
    bias = jnp.broadcast_to(up_bias.astype(jnp.float32), (8, slice_out))
    anywhere = pl.BlockSpec(memory_space=pl.ANY)
    vmem = pl.BlockSpec(memory_space=pltpu.VMEM)
    dma = pltpu.SemaphoreType.DMA
    fine = pl.pallas_call(
        functools.partial(kernel, chips),
        out_shape=jax.ShapeDtypeStruct((rows, 2, width, 2 * decoded), jnp.bfloat16),
        in_specs=[anywhere] * 3 + [vmem] * 4,
        out_specs=vmem,
        scratch_shapes=[
            pltpu.VMEM((devices, rows, width, channels), jnp.bfloat16),
            pltpu.VMEM((9 * outputs, channels), jnp.bfloat16),
            pltpu.VMEM((TAPS, devices, slice_out, channels), jnp.bfloat16),
            pltpu.VMEM((devices * rows + 2, width, outputs), jnp.float32),
            pltpu.VMEM((devices, rows * width, outputs), jnp.bfloat16),
            pltpu.VMEM((devices, rows * width, outputs), jnp.bfloat16),
            pltpu.VMEM((8, decoded), jnp.float32),
            pltpu.VMEM((devices, 8, decoded), jnp.float32),
            dma((2 + TAPS,)),
            dma((2, chips, rows)),
            dma((chips, rows)),
            dma((devices, rows)),
            dma((2, chips)),
            dma((TAPS - 1, chips)),
            dma((chips, TAPS)),
            dma((devices, TAPS)),
            dma((devices,)),
            dma((devices,)),
            dma((devices,)),
            dma((devices,)),
        ],
        compiler_params=pltpu.CompilerParams(
            collective_id=0, has_side_effects=True, vmem_limit_bytes=48 * 1024 * 1024
        ),
    )(
        coarse,
        conv_w,
        up_w,
        conv_bias.reshape(1, outputs),
        norm_gain.reshape(1, outputs),
        norm_shift.reshape(1, outputs),
        bias,
    )
    return fine.reshape(2 * rows, 2 * width, decoded)


def solution(mesh):
    return jax.shard_map(
        functools.partial(body, mesh.shape["sp"] // 2),
        mesh=mesh,
        in_specs=(
            P(("grp", "sp"), None, None),
            P("sp", None, None, None),
            P("sp"),
            P("sp"),
            P("sp"),
            P("sp", None, None, None),
            P("sp"),
        ),
        out_specs=P(("grp", "sp"), None, None),
        check_vma=False,
    )
```

time: 106 us -> 50.3 us (0.47)
  waiting for transfers between devices: 54.9 us -> 0 us
  Pallas kernels: 0 us -> 42.7 us
  blocking collectives: 19 us -> 0 us
  between operations: 13.6 us -> 0.03 us
  matrix products: 5.45 us -> 0 us
  local copies, waits for them, and re-layouts: 10.2 us -> 7.28 us
  other arithmetic: 1.51 us -> 0 us
    all_gather x2 -> x0, waiting for transfers between devices: 54.2 us -> none  [the longest x1 27.3 us: full_conv(): lax.all_gather(coarse, 'sp', axis=0, tiled=True)]
    pallas_call x0 -> x1, Pallas kernels: none -> 42.7 us  [body(): pl.pallas_call(functools.partial(kernel, chips), out_shape=jax.ShapeDtype...]
    all_to_all x1 -> x0, blocking collectives: 19 us -> none  [body(): lax.all_to_all(decoded, 'sp', split_axis=0, concat_axis=2, tiled=True)]
    slice x3 -> x0, local copies, waits for them, and re-layouts: 6.28 us -> none  [the longest x1 3.53 us: conv_rows(): padded[:, offset:offset + width_cols, :]]
    dot_general x4 -> x0, matrix products: 5.45 us -> none  [the longest x3 3.02 us: conv_rows(): jnp.dot(window, weights_cat[offset], preferred_element_type=jnp.float32)]
    unnamed x12 -> x10, local copies, waits for them, and re-layouts: 0.81 us -> 4.55 us
    transpose x0 -> x1, local copies, waits for them, and re-layouts: none -> 1.2 us  [body(): jnp.transpose(up_weight, (1, 2, 0, 3)).reshape(TAPS, slice_out, channels)]
  transfers between devices with their start and end apart: 2 -> 0, of which waited for: 2 -> 0; matrix products, arithmetic and copies ran while one was open for 2% -> 0% of each run, Pallas kernels for 0% -> 0%
where the time goes in v1:
time: 50.3 us; the launch traced here: 50.1 us
  Pallas kernels  42.7 us (85%)
  local copies, waits for them, and re-layouts  7.28 us (14%)
    pallas_call x1, Pallas kernels, body(): pl.pallas_call(functools.partial(kernel, chips), out_shape=jax.ShapeDtype...  42.7 us
    unnamed x10, local copies, waits for them, and re-layouts  4.55 us
    transpose x1, local copies, waits for them, and re-layouts, body(): jnp.transpose(up_weight, (1, 2, 0, 3)).reshape(TAPS, slice_out, channels)  1.2 us

profile of v1, /device:TPU:1, one launch (start us, length us, event | category | flops | bytes accessed | tf_op | source)
XLA Modules:
  0.0 50.1 jit_solution(17248225372277891874)
XLA Ops:
  0.0 0.7 %broadcast_in_dim.3.up_bias = f32[8,64]{1,0:T(8,128)S(1)} broadcast(bf16[64]{0:T(256)(128)(2,1)} %param.13), dimensions={1} | broadcast | bytes 2176 | tf_op jit(solution)/shard_map/broadcast_in_dim | solution.py:365
  0.7 1.2 %copy.8 = bf16[2,2,64,1024]{3,2,1,0:T(8,128)(2,1)S(1)} copy(bf16[2,2,64,1024]{3,1,0,2:T(2,128)(2,1)} %bitcast.15) | data formatting | bytes 1048576 | tf_op jit(solution)/shard_map/transpose | solution.py:364
  1.9 0.0 copy-start
  1.9 1.7 %copy-done = bf16[128,3,3,1024]{3,0,2,1:T(8,128)(2,1)S(1)} copy-done((bf16[128,3,3,1024]{3,0,2,1:T(8,128)(2,1)S(1)}, bf16[128,3,3,1024]{3,0,2,1:T(8,128)(2,1)}, u32[]{:S(2)}) %copy-start) | copy-done | bytes 2359320
  3.5 0.0 copy-start.1
  3.5 0.9 %copy-done.1 = bf16[2,48,1024]{2,1,0:T(8,128)(2,1)S(1)} copy-done((bf16[2,48,1024]{2,1,0:T(8,128)(2,1)S(1)}, bf16[2,48,1024]{2,1,0:T(8,128)(2,1)}, u32[]{:S(2)}) %copy-start.1) | copy-done | bytes 196632
  4.5 0.0 copy-start.2
  4.5 0.7 %copy-done.2 = f32[128]{0:T(128)S(1)} copy-done((f32[128]{0:T(128)S(1)}, f32[128]{0:T(128)}, u32[]{:S(2)}) %copy-start.2) | copy-done | bytes 536
  5.1 0.0 copy-start.3
  5.1 0.7 %copy-done.3 = f32[128]{0:T(128)S(1)} copy-done((f32[128]{0:T(128)S(1)}, f32[128]{0:T(128)}, u32[]{:S(2)}) %copy-start.3) | copy-done | bytes 536
  5.8 0.0 copy-start.4
  5.8 0.7 %copy-done.4 = f32[128]{0:T(128)S(1)} copy-done((f32[128]{0:T(128)S(1)}, f32[128]{0:T(128)}, u32[]{:S(2)}) %copy-start.4) | copy-done | bytes 536
  6.4 42.7 %shard_map.73 = bf16[2,2,48,1024]{3,2,1,0:T(8,128)(2,1)S(1)} custom-call(bf16[2,48,1024]{2,1,0:T(8,128)(2,1)S(1)} %copy-done.1, bf16[1152,1024]{1,0:T(8,128)(2,1)S(1)} %bitcast.10, bf16[4,64,1024]{2,1,0:T(8,128)(2,1)S(1)} %bitcast.11, f32[1,128]{1,0:T(1,128)S(1)} %bitcast.12, f32[1,128]{1,0:T(1,128)S(1)} %bitcast.13, f32[1,128]{1,0:T(1,128)S(1)} %bitcast.14, ...), custom_call_target="tpu_custom_call" | custom-call | tf_op jit(solution)/shard_map/pallas_call | solution.py:369
  49.2 0.9 %reshape.23 = bf16[4,96,512]{2,1,0:T(8,128)(2,1)} reshape(bf16[2,2,48,1024]{3,2,1,0:T(8,128)(2,1)S(1)} %shard_map.73) | data formatting | bytes 786432 | tf_op jit(solution)/shard_map/reshape | solution.py:408
Async XLA Ops:
  1.9 1.7 %copy-start = (bf16[128,3,3,1024]{3,0,2,1:T(8,128)(2,1)S(1)}, bf16[128,3,3,1024]{3,0,2,1:T(8,128)(2,1)}, u32[]{:S(2)}) copy-start(bf16[128,3,3,1024]{3,0,2,1:T(8,128)(2,1)} %param.8) | copy-start | bytes 7077892
  3.5 0.9 %copy-start.1 = (bf16[2,48,1024]{2,1,0:T(8,128)(2,1)S(1)}, bf16[2,48,1024]{2,1,0:T(8,128)(2,1)}, u32[]{:S(2)}) copy-start(bf16[2,48,1024]{2,1,0:T(8,128)(2,1)} %coarse.1) | copy-start | bytes 589828
  4.5 0.7 %copy-start.2 = (f32[128]{0:T(128)S(1)}, f32[128]{0:T(128)}, u32[]{:S(2)}) copy-start(f32[128]{0:T(128)} %param.9) | copy-start | bytes 1540
  5.1 0.7 %copy-start.3 = (f32[128]{0:T(128)S(1)}, f32[128]{0:T(128)}, u32[]{:S(2)}) copy-start(f32[128]{0:T(128)} %param.10) | copy-start | bytes 1540
  5.8 0.7 %copy-start.4 = (f32[128]{0:T(128)S(1)}, f32[128]{0:T(128)}, u32[]{:S(2)}) copy-start(f32[128]{0:T(128)} %param.11) | copy-start | bytes 1540

commit v2 on v1

--- a/solution.py
+++ b/solution.py
@@ -17,9 +17,9 @@
     coarse,
     conv_w,
     up_w,
-    conv_bias,
-    gain,
-    shift,
+    bias_hbm,
+    gain_hbm,
+    shift_hbm,
     up_bias,
     out,
     gathered,
@@ -30,6 +30,9 @@
     act_all,
     bias_own,
     bias_all,
+    conv_bias,
+    gain,
+    shift,
     local_sem,
     c_line,
     c_sib,
@@ -87,10 +90,9 @@
     def coarse_wait(b, h):
         remote(gathered.at[b, h], gathered.at[b, h], c_sib.at[0, h], c_recv.at[b, h], at(col, sibling)).wait_recv()
 
-    def up_line(direction, src, ref):
-        b = 2 * src + core
-        target = 2 * onward(direction)[0] + core
-        return remote(ref, up_all.at[part, b], u_line.at[direction, src], u_recv.at[b, part], at(col, target))
+    def up_direct(chip):
+        target = 2 * chip + core
+        return remote(up_w.at[part], up_all.at[part, me], u_line.at[chip], u_recv.at[me, part], at(col, target))
 
     def up_xy(q, src):
         b = 2 * src + core
@@ -110,9 +112,11 @@
     up_copies = [
         pltpu.make_async_copy(up_w.at[tap], up_all.at[tap, me], local_sem.at[2 + tap]) for tap in range(TAPS)
     ]
-    w_copy.start()
-    own_copy.start()
-    for copy in up_copies:
+    small = [
+        pltpu.make_async_copy(src, dst, local_sem.at[2 + TAPS + i])
+        for i, (src, dst) in enumerate(((bias_hbm, conv_bias), (gain_hbm, gain), (shift_hbm, shift)))
+    ]
+    for copy in [own_copy, w_copy] + up_copies + small:
         copy.start()
 
     barrier = pltpu.get_barrier_semaphore()
@@ -137,12 +141,18 @@
                 coarse_line(direction, z, h, coarse.at[h]).start()
 
         coarse_sib(z, h, coarse.at[h]).start()
-    for direction in range(2):
-
-        @pl.when(onward(direction)[1])
-        def _():
-            up_line(direction, z, up_w.at[part]).start()
-
+
+    def send_up(k, carry):
+        for direction in range(2):
+            chip, there = origin(direction, k)
+
+            @pl.when(there)
+            def _():
+                up_direct(chip).start()
+
+        return carry
+
+    lax.fori_loop(1, chips, send_up, 0)
     for tap in range(TAPS):
         up_sib(z, tap, up_w.at[tap]).start()
 
@@ -228,11 +238,6 @@
             def _():
                 b = 2 * src + core
                 up_wait(b, part)
-
-                @pl.when(onward(direction)[1])
-                def _():
-                    up_line(direction, src, up_all.at[part, b]).start()
-
                 for q in range(1, TAPS):
                     up_xy(q, src).start()
                 up_sib(src, part, up_all.at[part, b]).start()
@@ -255,6 +260,8 @@
     lax.fori_loop(1, chips, step, 0)
 
     height = devices * rows
+    for copy in small:
+        copy.wait()
     values = summed[1 : height + 1].reshape(height * width, outputs) + conv_bias[...]
     scale = 1.0 / (height * width * GSIZE)
     same = (
@@ -329,6 +336,7 @@
 
         @pl.when(src != z)
         def _():
+            up_direct(src).wait_send()
             for q in range(1, TAPS):
                 up_xy(q, src).wait_send()
 
@@ -339,7 +347,6 @@
             def _():
                 for h in range(rows):
                     coarse_line(direction, src, h, gathered.at[0, h]).wait_send()
-                up_line(direction, src, up_all.at[0, 0]).wait_send()
 
         return carry
 
@@ -363,13 +370,13 @@
     conv_w = jnp.transpose(conv_weight, (1, 2, 0, 3)).reshape(9 * outputs, channels)
     up_w = jnp.transpose(up_weight, (1, 2, 0, 3)).reshape(TAPS, slice_out, channels)
     bias = jnp.broadcast_to(up_bias.astype(jnp.float32), (8, slice_out))
-    anywhere = pl.BlockSpec(memory_space=pl.ANY)
+    hbm = pl.BlockSpec(memory_space=pltpu.HBM)
     vmem = pl.BlockSpec(memory_space=pltpu.VMEM)
     dma = pltpu.SemaphoreType.DMA
     fine = pl.pallas_call(
         functools.partial(kernel, chips),
         out_shape=jax.ShapeDtypeStruct((rows, 2, width, 2 * decoded), jnp.bfloat16),
-        in_specs=[anywhere] * 3 + [vmem] * 4,
+        in_specs=[hbm] * 6 + [vmem],
         out_specs=vmem,
         scratch_shapes=[
             pltpu.VMEM((devices, rows, width, channels), jnp.bfloat16),
@@ -380,11 +387,14 @@
             pltpu.VMEM((devices, rows * width, outputs), jnp.bfloat16),
             pltpu.VMEM((8, decoded), jnp.float32),
             pltpu.VMEM((devices, 8, decoded), jnp.float32),
-            dma((2 + TAPS,)),
+            pltpu.VMEM((1, outputs), jnp.float32),
+            pltpu.VMEM((1, outputs), jnp.float32),
+            pltpu.VMEM((1, outputs), jnp.float32),
+            dma((5 + TAPS,)),
             dma((2, chips, rows)),
             dma((chips, rows)),
             dma((devices, rows)),
-            dma((2, chips)),
+            dma((chips,)),
             dma((TAPS - 1, chips)),
             dma((chips, TAPS)),
             dma((devices, TAPS)),
@@ -394,7 +404,7 @@
             dma((devices,)),
         ],
         compiler_params=pltpu.CompilerParams(
-            collective_id=0, has_side_effects=True, vmem_limit_bytes=48 * 1024 * 1024
+            collective_id=0, has_side_effects=True, vmem_limit_bytes=60 * 1024 * 1024
         ),
     )(
         coarse,

time: 50.3 us -> 51.5 us (1.024)
  Pallas kernels: 42.7 us -> 46.1 us
  local copies, waits for them, and re-layouts: 7.28 us -> 5.11 us
    unnamed x10 -> x0, local copies, waits for them, and re-layouts: 4.55 us -> none
    pallas_call x1, Pallas kernels: 42.7 us -> 46.1 us  [body(): pl.pallas_call(functools.partial(kernel, chips), out_shape=jax.ShapeDtype...]
    reshape x1, local copies, waits for them, and re-layouts: 0.88 us -> 1.87 us  [body(): return fine.reshape(2 * rows, 2 * width, decoded)]
    transpose x1, local copies, waits for them, and re-layouts: 1.2 us -> 1.99 us  [body(): jnp.transpose(up_weight, (1, 2, 0, 3)).reshape(TAPS, slice_out, channels)]
    broadcast_in_dim x1, local copies, waits for them, and re-layouts: 0.66 us -> 1.25 us  [body(): bias = jnp.broadcast_to(up_bias.astype(jnp.float32), (8, slice_out))]
where the time goes in v2:
time: 51.5 us; the launch traced here: 51.2 us
  Pallas kernels  46.1 us (90%)
  local copies, waits for them, and re-layouts  5.11 us (10%)
    pallas_call x1, Pallas kernels, body(): pl.pallas_call(functools.partial(kernel, chips), out_shape=jax.ShapeDtype...  46.1 us
    transpose x1, local copies, waits for them, and re-layouts, body(): jnp.transpose(up_weight, (1, 2, 0, 3)).reshape(TAPS, slice_out, channels)  1.99 us
    reshape x1, local copies, waits for them, and re-layouts, body(): return fine.reshape(2 * rows, 2 * width, decoded)  1.87 us
    broadcast_in_dim x1, local copies, waits for them, and re-layouts, body(): bias = jnp.broadcast_to(up_bias.astype(jnp.float32), (8, slice_out))  1.25 us

profile of v2, /device:TPU:1, one launch (start us, length us, event | category | flops | bytes accessed | tf_op | source)
XLA Modules:
  0.0 51.2 jit_solution(3364168312852141657)
XLA Ops:
  0.0 1.2 %broadcast_in_dim.3.up_bias = f32[8,64]{1,0:T(8,128)} broadcast(bf16[64]{0:T(256)(128)(2,1)} %param.13), dimensions={1} | broadcast | bytes 2176 | tf_op jit(solution)/shard_map/broadcast_in_dim | solution.py:372
  1.2 2.0 %copy.8 = bf16[2,2,64,1024]{3,2,1,0:T(8,128)(2,1)} copy(bf16[2,2,64,1024]{3,1,0,2:T(2,128)(2,1)} %bitcast.12) | data formatting | bytes 1048576 | tf_op jit(solution)/shard_map/transpose | solution.py:371
  3.2 46.1 %shard_map.73 = bf16[2,2,48,1024]{3,2,1,0:T(8,128)(2,1)} custom-call(bf16[2,48,1024]{2,1,0:T(8,128)(2,1)} %coarse.1, bf16[1152,1024]{1,0:T(8,128)(2,1)} %bitcast.10, bf16[4,64,1024]{2,1,0:T(8,128)(2,1)} %bitcast.11, f32[1,128]{1,0:T(1,128)} %bitcast.13, f32[1,128]{1,0:T(1,128)} %bitcast.14, f32[1,128]{1,0:T(1,128)} %bitcast.15, f32[8,64]{1,0:T(8,128)} %broadcast_in_dim.3.up_bias), custom_call_target="tpu_custom_call" | custom-call | tf_op jit(solution)/shard_map/pallas_call | solution.py:376
  49.4 1.9 %reshape.23 = bf16[4,96,512]{2,1,0:T(8,128)(2,1)} reshape(bf16[2,2,48,1024]{3,2,1,0:T(8,128)(2,1)} %shard_map.73) | data formatting | bytes 786432 | tf_op jit(solution)/shard_map/reshape | solution.py:418

commit v3 on v2

--- a/solution.py
+++ b/solution.py
@@ -33,6 +33,8 @@
     conv_bias,
     gain,
     shift,
+    mixed,
+    bias_raw,
     local_sem,
     c_line,
     c_sib,
@@ -90,9 +92,10 @@
     def coarse_wait(b, h):
         remote(gathered.at[b, h], gathered.at[b, h], c_sib.at[0, h], c_recv.at[b, h], at(col, sibling)).wait_recv()
 
-    def up_direct(chip):
-        target = 2 * chip + core
-        return remote(up_w.at[part], up_all.at[part, me], u_line.at[chip], u_recv.at[me, part], at(col, target))
+    def up_line(direction, src, ref):
+        b = 2 * src + core
+        target = 2 * onward(direction)[0] + core
+        return remote(ref, up_all.at[part, b], u_line.at[direction, src], u_recv.at[b, part], at(col, target))
 
     def up_xy(q, src):
         b = 2 * src + core
@@ -116,7 +119,8 @@
         pltpu.make_async_copy(src, dst, local_sem.at[2 + TAPS + i])
         for i, (src, dst) in enumerate(((bias_hbm, conv_bias), (gain_hbm, gain), (shift_hbm, shift)))
     ]
-    for copy in [own_copy, w_copy] + up_copies + small:
+    bias_copy_in = pltpu.make_async_copy(up_bias, bias_raw, local_sem.at[5 + TAPS])
+    for copy in [own_copy, w_copy, bias_copy_in] + up_copies + small:
         copy.start()
 
     barrier = pltpu.get_barrier_semaphore()
@@ -141,25 +145,15 @@
                 coarse_line(direction, z, h, coarse.at[h]).start()
 
         coarse_sib(z, h, coarse.at[h]).start()
-
-    def send_up(k, carry):
-        for direction in range(2):
-            chip, there = origin(direction, k)
-
-            @pl.when(there)
-            def _():
-                up_direct(chip).start()
-
-        return carry
-
-    lax.fori_loop(1, chips, send_up, 0)
     for tap in range(TAPS):
         up_sib(z, tap, up_w.at[tap]).start()
 
     lanes = lax.broadcasted_iota(jnp.int32, (slice_out, decoded), 1)
     line = lax.broadcasted_iota(jnp.int32, (slice_out, decoded), 0)
     chosen = (lanes == line + me * slice_out).astype(jnp.float32)
-    placed = jnp.dot(up_bias[...], chosen, preferred_element_type=jnp.float32, precision=lax.Precision.HIGHEST)
+    bias_copy_in.wait()
+    raw = jnp.broadcast_to(bias_raw[...].astype(jnp.float32).reshape(1, slice_out), (8, slice_out))
+    placed = jnp.dot(raw, chosen, preferred_element_type=jnp.float32, precision=lax.Precision.HIGHEST)
     bias_own[...] = placed
     bias_all[me] = placed
 
@@ -204,6 +198,14 @@
         coarse_wait(sibling, h)
     conv_pair(z)
 
+    for direction in range(2):
+
+        @pl.when(onward(direction)[1])
+        def _():
+            for h in range(rows):
+                coarse_line(direction, z, h, coarse.at[h]).wait_send()
+            up_line(direction, z, up_w.at[part]).start()
+
     def spread(k):
         for direction in range(2):
             src, there = origin(direction, k)
@@ -215,6 +217,23 @@
                     up_wait(2 * src + core, tap)
                     up_sib(src, tap, up_all.at[tap, 2 * src + core]).start()
 
+    def pass_up(k):
+        for direction in range(2):
+            src, there = origin(direction, k)
+
+            @pl.when(there)
+            def _():
+                b = 2 * src + core
+                up_wait(b, part)
+
+                @pl.when(onward(direction)[1])
+                def _():
+                    up_line(direction, src, up_all.at[part, b]).start()
+
+                for q in range(1, TAPS):
+                    up_xy(q, src).start()
+                up_sib(src, part, up_all.at[part, b]).start()
+
     def step(k, carry):
         for direction in range(2):
             src, there = origin(direction, k)
@@ -231,16 +250,9 @@
 
                     coarse_sib(src, h, gathered.at[b, h]).start()
 
-        for direction in range(2):
-            src, there = origin(direction, k)
-
-            @pl.when(there)
-            def _():
-                b = 2 * src + core
-                up_wait(b, part)
-                for q in range(1, TAPS):
-                    up_xy(q, src).start()
-                up_sib(src, part, up_all.at[part, b]).start()
+        @pl.when(k > 1)
+        def _():
+            pass_up(k - 1)
 
         for direction in range(2):
             src, there = origin(direction, k)
@@ -251,9 +263,9 @@
                     coarse_wait(2 * src + 1 - core, h)
                 conv_pair(src)
 
-        @pl.when(k > 1)
+        @pl.when(k > 2)
         def _():
-            spread(k - 1)
+            spread(k - 2)
 
         return carry
 
@@ -289,6 +301,9 @@
     lax.fori_loop(1, devices, send_act, 0)
     act_all[me] = act[me]
 
+    pass_up(chips - 1)
+    if chips > 2:
+        spread(chips - 2)
     spread(chips - 1)
 
     def arrivals(i, carry):
@@ -324,9 +339,12 @@
                     preferred_element_type=jnp.float32,
                 )
         a, b = tap // 2, tap % 2
-        out[:, a, :, b * decoded : (b + 1) * decoded] = (
-            (fine + bias).astype(jnp.bfloat16).reshape(rows, width, decoded)
-        )
+        for i in range(rows):
+            values = fine[i * width : (i + 1) * width] + bias
+            for t in range(decoded // 128):
+                mixed[t, 2 * i + a, pl.ds(b, width, stride=2), :] = values[:, 128 * t : 128 * (t + 1)]
+    for t in range(decoded // 128):
+        out[:, :, 128 * t : 128 * (t + 1)] = mixed[t].astype(jnp.bfloat16)
 
     def sent(src, carry):
         for h in range(rows):
@@ -336,7 +354,6 @@
 
         @pl.when(src != z)
         def _():
-            up_direct(src).wait_send()
             for q in range(1, TAPS):
                 up_xy(q, src).wait_send()
 
@@ -345,8 +362,12 @@
 
             @pl.when(jnp.logical_and(passed, onward(direction)[1]))
             def _():
-                for h in range(rows):
-                    coarse_line(direction, src, h, gathered.at[0, h]).wait_send()
+                @pl.when(src != z)
+                def _():
+                    for h in range(rows):
+                        coarse_line(direction, src, h, gathered.at[0, h]).wait_send()
+
+                up_line(direction, src, up_all.at[0, 0]).wait_send()
 
         return carry
 
@@ -369,14 +390,13 @@
     decoded = devices * slice_out
     conv_w = jnp.transpose(conv_weight, (1, 2, 0, 3)).reshape(9 * outputs, channels)
     up_w = jnp.transpose(up_weight, (1, 2, 0, 3)).reshape(TAPS, slice_out, channels)
-    bias = jnp.broadcast_to(up_bias.astype(jnp.float32), (8, slice_out))
     hbm = pl.BlockSpec(memory_space=pltpu.HBM)
     vmem = pl.BlockSpec(memory_space=pltpu.VMEM)
     dma = pltpu.SemaphoreType.DMA
-    fine = pl.pallas_call(
+    return pl.pallas_call(
         functools.partial(kernel, chips),
-        out_shape=jax.ShapeDtypeStruct((rows, 2, width, 2 * decoded), jnp.bfloat16),
-        in_specs=[hbm] * 6 + [vmem],
+        out_shape=jax.ShapeDtypeStruct((2 * rows, 2 * width, decoded), jnp.bfloat16),
+        in_specs=[hbm, hbm, pl.BlockSpec(memory_space=pl.ANY), hbm, hbm, hbm, hbm],
         out_specs=vmem,
         scratch_shapes=[
             pltpu.VMEM((devices, rows, width, channels), jnp.bfloat16),
@@ -390,11 +410,13 @@
             pltpu.VMEM((1, outputs), jnp.float32),
             pltpu.VMEM((1, outputs), jnp.float32),
             pltpu.VMEM((1, outputs), jnp.float32),
-            dma((5 + TAPS,)),
+            pltpu.VMEM((decoded // 128, 2 * rows, 2 * width, 128), jnp.float32),
+            pltpu.VMEM((slice_out,), jnp.bfloat16),
+            dma((6 + TAPS,)),
             dma((2, chips, rows)),
             dma((chips, rows)),
             dma((devices, rows)),
-            dma((chips,)),
+            dma((2, chips)),
             dma((TAPS - 1, chips)),
             dma((chips, TAPS)),
             dma((devices, TAPS)),
@@ -413,9 +435,8 @@
         conv_bias.reshape(1, outputs),
         norm_gain.reshape(1, outputs),
         norm_shift.reshape(1, outputs),
-        bias,
+        up_bias,
     )
-    return fine.reshape(2 * rows, 2 * width, decoded)
 
 
 def solution(mesh):

time: 51.5 us -> 49.5 us (0.961)
  local copies, waits for them, and re-layouts: 5.11 us -> 3.76 us
  Pallas kernels: 46.1 us -> 45.5 us
    reshape x1 -> x0, local copies, waits for them, and re-layouts: 1.87 us -> none  [body(): return fine.reshape(2 * rows, 2 * width, decoded)]
    unnamed x0 -> x1, local copies, waits for them, and re-layouts: none -> 1.77 us
    broadcast_in_dim x1 -> x0, local copies, waits for them, and re-layouts: 1.25 us -> none  [body(): bias = jnp.broadcast_to(up_bias.astype(jnp.float32), (8, slice_out))]
    pallas_call x1, Pallas kernels: 46.1 us -> 45.5 us  [body(): pl.pallas_call(functools.partial(kernel, chips), out_shape=jax.ShapeDtype...]
where the time goes in v3:
time: 49.5 us; the launch traced here: 49.3 us
  Pallas kernels  45.5 us (92%)
  local copies, waits for them, and re-layouts  3.76 us (8%)
    pallas_call x1, Pallas kernels, body(): pl.pallas_call(functools.partial(kernel, chips), out_shape=jax.ShapeDtype...  45.5 us
    transpose x1, local copies, waits for them, and re-layouts, body(): jnp.transpose(up_weight, (1, 2, 0, 3)).reshape(TAPS, slice_out, channels)  1.99 us
    unnamed x1, local copies, waits for them, and re-layouts  1.77 us

profile of v3, /device:TPU:1, one launch (start us, length us, event | category | flops | bytes accessed | tf_op | source)
XLA Modules:
  0.0 49.3 jit_solution(12155846128118049051)
XLA Ops:
  0.0 2.0 %copy.8 = bf16[2,2,64,1024]{3,2,1,0:T(8,128)(2,1)} copy(bf16[2,2,64,1024]{3,1,0,2:T(2,128)(2,1)} %bitcast.10) | data formatting | bytes 1048576 | tf_op jit(solution)/shard_map/transpose | solution.py:392
  2.0 45.5 %shard_map.73 = bf16[4,96,512]{2,1,0:T(8,128)(2,1)} custom-call(bf16[2,48,1024]{2,1,0:T(8,128)(2,1)} %coarse.1, bf16[1152,1024]{1,0:T(8,128)(2,1)} %bitcast.8, bf16[4,64,1024]{2,1,0:T(8,128)(2,1)} %bitcast.9, f32[1,128]{1,0:T(1,128)} %bitcast.11, f32[1,128]{1,0:T(1,128)} %bitcast.12, f32[1,128]{1,0:T(1,128)} %bitcast.13, bf16[64]{0:T(256)(128)(2,1)} %up_bias.1), custom_call_target="tpu_custom_call" | custom-call | tf_op jit(solution)/shard_map/pallas_call | solution.py:396
  47.5 1.8 %copy.10 = bf16[4,96,512]{2,1,0:T(8,128)(2,1)} copy(bf16[4,96,512]{2,1,0:T(8,128)(2,1)} %shard_map.73) | data formatting | bytes 786432

commit v4 on v3

--- a/solution.py
+++ b/solution.py
@@ -43,6 +43,7 @@
     u_xy,
     u_sib,
     u_recv,
+    u_whole,
     b_send,
     b_recv,
     a_send,
@@ -102,13 +103,13 @@
         ref = up_all.at[part, b]
         return remote(ref, ref, u_xy.at[q - 1, src], u_recv.at[b, part], at(base + (part + q) % TAPS, me))
 
-    def up_sib(src, tap, ref):
+    def up_sib(src, ref):
         b = 2 * src + core
-        return remote(ref, up_all.at[tap, b], u_sib.at[src, tap], u_recv.at[b, tap], at(col, sibling))
+        return remote(ref, up_all.at[:, b], u_sib.at[src], u_whole.at[b], at(col, sibling))
 
     def up_wait(b, tap):
         ref = up_all.at[tap, b]
-        remote(ref, ref, u_sib.at[0, tap], u_recv.at[b, tap], at(col, sibling)).wait_recv()
+        remote(ref, ref, u_xy.at[0, 0], u_recv.at[b, tap], at(col, sibling)).wait_recv()
 
     w_copy = pltpu.make_async_copy(conv_w, w_vmem, local_sem.at[0])
     own_copy = pltpu.make_async_copy(coarse, gathered.at[me], local_sem.at[1])
@@ -145,8 +146,13 @@
                 coarse_line(direction, z, h, coarse.at[h]).start()
 
         coarse_sib(z, h, coarse.at[h]).start()
-    for tap in range(TAPS):
-        up_sib(z, tap, up_w.at[tap]).start()
+    for direction in range(2):
+
+        @pl.when(onward(direction)[1])
+        def _():
+            up_line(direction, z, up_w.at[part]).start()
+
+    up_sib(z, up_w).start()
 
     lanes = lax.broadcasted_iota(jnp.int32, (slice_out, decoded), 1)
     line = lax.broadcasted_iota(jnp.int32, (slice_out, decoded), 0)
@@ -198,14 +204,6 @@
         coarse_wait(sibling, h)
     conv_pair(z)
 
-    for direction in range(2):
-
-        @pl.when(onward(direction)[1])
-        def _():
-            for h in range(rows):
-                coarse_line(direction, z, h, coarse.at[h]).wait_send()
-            up_line(direction, z, up_w.at[part]).start()
-
     def spread(k):
         for direction in range(2):
             src, there = origin(direction, k)
@@ -215,7 +213,7 @@
                 for q in range(1, TAPS):
                     tap = (part + q) % TAPS
                     up_wait(2 * src + core, tap)
-                    up_sib(src, tap, up_all.at[tap, 2 * src + core]).start()
+                up_sib(src, up_all.at[:, 2 * src + core]).start()
 
     def pass_up(k):
         for direction in range(2):
@@ -232,7 +230,6 @@
 
                 for q in range(1, TAPS):
                     up_xy(q, src).start()
-                up_sib(src, part, up_all.at[part, b]).start()
 
     def step(k, carry):
         for direction in range(2):
@@ -250,9 +247,7 @@
 
                     coarse_sib(src, h, gathered.at[b, h]).start()
 
-        @pl.when(k > 1)
-        def _():
-            pass_up(k - 1)
+        pass_up(k)
 
         for direction in range(2):
             src, there = origin(direction, k)
@@ -263,9 +258,9 @@
                     coarse_wait(2 * src + 1 - core, h)
                 conv_pair(src)
 
-        @pl.when(k > 2)
+        @pl.when(k > 1)
         def _():
-            spread(k - 2)
+            spread(k - 1)
 
         return carry
 
@@ -301,27 +296,51 @@
     lax.fori_loop(1, devices, send_act, 0)
     act_all[me] = act[me]
 
-    pass_up(chips - 1)
-    if chips > 2:
-        spread(chips - 2)
+    def early(i, carry):
+        other = lax.rem(me + i, devices)
+        bias_copy(other, other).wait()
+        return carry
+
+    lax.fori_loop(1, devices, early, 0)
+
+    def coarse_sent(src, carry):
+        for h in range(rows):
+            coarse_sib(src, h, gathered.at[0, h]).wait_send()
+        for direction in range(2):
+            passed = src <= z if direction == 0 else src >= z
+
+            @pl.when(jnp.logical_and(passed, onward(direction)[1]))
+            def _():
+                for h in range(rows):
+                    coarse_line(direction, src, h, gathered.at[0, h]).wait_send()
+                up_line(direction, src, up_all.at[0, 0]).wait_send()
+
+        return carry
+
+    lax.fori_loop(0, chips, coarse_sent, 0)
     spread(chips - 1)
+    for copy in up_copies:
+        copy.wait()
 
     def arrivals(i, carry):
         other = lax.rem(me + i, devices)
-        bias_copy(other, other).wait_recv()
-        act_copy(other, other).wait_recv()
+        act_copy(other, other).wait()
         return carry
 
     lax.fori_loop(1, devices, arrivals, 0)
 
     def up_arrivals(src, carry):
-        for tap in range(TAPS):
-            up_wait(2 * src + 1 - core, tap)
+        @pl.when(src != z)
+        def _():
+            for q in range(1, TAPS):
+                up_xy(q, src).wait_send()
+
+        up_sib(src, up_all.at[:, 0]).wait_send()
+        b = 2 * src + 1 - core
+        remote(up_all.at[:, b], up_all.at[:, b], u_sib.at[src], u_whole.at[b], at(col, sibling)).wait_recv()
         return carry
 
     lax.fori_loop(0, chips, up_arrivals, 0)
-    for copy in up_copies:
-        copy.wait()
 
     bias = jnp.sum(bias_all[...], axis=0)[:1]
     for tap in range(TAPS):
@@ -345,41 +364,6 @@
                 mixed[t, 2 * i + a, pl.ds(b, width, stride=2), :] = values[:, 128 * t : 128 * (t + 1)]
     for t in range(decoded // 128):
         out[:, :, 128 * t : 128 * (t + 1)] = mixed[t].astype(jnp.bfloat16)
-
-    def sent(src, carry):
-        for h in range(rows):
-            coarse_sib(src, h, gathered.at[0, h]).wait_send()
-        for tap in range(TAPS):
-            up_sib(src, tap, up_all.at[tap, 0]).wait_send()
-
-        @pl.when(src != z)
-        def _():
-            for q in range(1, TAPS):
-                up_xy(q, src).wait_send()
-
-        for direction in range(2):
-            passed = src <= z if direction == 0 else src >= z
-
-            @pl.when(jnp.logical_and(passed, onward(direction)[1]))
-            def _():
-                @pl.when(src != z)
-                def _():
-                    for h in range(rows):
-                        coarse_line(direction, src, h, gathered.at[0, h]).wait_send()
-
-                up_line(direction, src, up_all.at[0, 0]).wait_send()
-
-        return carry
-
-    lax.fori_loop(0, chips, sent, 0)
-
-    def small_sent(i, carry):
-        other = lax.rem(me + i, devices)
-        bias_copy(other, other).wait_send()
-        act_copy(other, other).wait_send()
-        return carry
-
-    lax.fori_loop(1, devices, small_sent, 0)
 
 
 def body(chips, coarse, conv_weight, conv_bias, norm_gain, norm_shift, up_weight, up_bias):
@@ -418,8 +402,9 @@
             dma((devices, rows)),
             dma((2, chips)),
             dma((TAPS - 1, chips)),
-            dma((chips, TAPS)),
+            dma((chips,)),
             dma((devices, TAPS)),
+            dma((devices,)),
             dma((devices,)),
             dma((devices,)),
             dma((devices,)),

time: 49.5 us -> 46.7 us (0.943)
  Pallas kernels: 45.5 us -> 42.7 us
    pallas_call x1, Pallas kernels: 45.5 us -> 42.7 us  [body(): pl.pallas_call(functools.partial(kernel, chips), out_shape=jax.ShapeDtype...]
where the time goes in v4:
time: 46.7 us; the launch traced here: 46.4 us
  Pallas kernels  42.7 us (91%)
  local copies, waits for them, and re-layouts  3.76 us (8%)
    pallas_call x1, Pallas kernels, body(): pl.pallas_call(functools.partial(kernel, chips), out_shape=jax.ShapeDtype...  42.7 us
    transpose x1, local copies, waits for them, and re-layouts, body(): jnp.transpose(up_weight, (1, 2, 0, 3)).reshape(TAPS, slice_out, channels)  1.99 us
    unnamed x1, local copies, waits for them, and re-layouts  1.77 us

profile of v4, /device:TPU:1, one launch (start us, length us, event | category | flops | bytes accessed | tf_op | source)
XLA Modules:
  0.0 46.4 jit_solution(7953066175135216612)
XLA Ops:
  0.0 2.0 %copy.8 = bf16[2,2,64,1024]{3,2,1,0:T(8,128)(2,1)} copy(bf16[2,2,64,1024]{3,1,0,2:T(2,128)(2,1)} %bitcast.10) | data formatting | bytes 1048576 | tf_op jit(solution)/shard_map/transpose | solution.py:376
  2.0 42.7 %shard_map.73 = bf16[4,96,512]{2,1,0:T(8,128)(2,1)} custom-call(bf16[2,48,1024]{2,1,0:T(8,128)(2,1)} %coarse.1, bf16[1152,1024]{1,0:T(8,128)(2,1)} %bitcast.8, bf16[4,64,1024]{2,1,0:T(8,128)(2,1)} %bitcast.9, f32[1,128]{1,0:T(1,128)} %bitcast.11, f32[1,128]{1,0:T(1,128)} %bitcast.12, f32[1,128]{1,0:T(1,128)} %bitcast.13, bf16[64]{0:T(256)(128)(2,1)} %up_bias.1), custom_call_target="tpu_custom_call" | custom-call | tf_op jit(solution)/shard_map/pallas_call | solution.py:380
  44.7 1.8 %copy.10 = bf16[4,96,512]{2,1,0:T(8,128)(2,1)} copy(bf16[4,96,512]{2,1,0:T(8,128)(2,1)} %shard_map.73) | data formatting | bytes 786432

commit v5 on v4

--- a/solution.py
+++ b/solution.py
@@ -247,7 +247,9 @@
 
                     coarse_sib(src, h, gathered.at[b, h]).start()
 
-        pass_up(k)
+        @pl.when(k < chips - 1)
+        def _():
+            pass_up(k)
 
         for direction in range(2):
             src, there = origin(direction, k)
@@ -258,7 +260,11 @@
                     coarse_wait(2 * src + 1 - core, h)
                 conv_pair(src)
 
-        @pl.when(k > 1)
+        @pl.when(k == chips - 1)
+        def _():
+            pass_up(k)
+
+        @pl.when(jnp.logical_and(k > 1, k < chips - 1))
         def _():
             spread(k - 1)
 
@@ -295,6 +301,9 @@
 
     lax.fori_loop(1, devices, send_act, 0)
     act_all[me] = act[me]
+
+    if chips > 2:
+        spread(chips - 2)
 
     def early(i, carry):
         other = lax.rem(me + i, devices)

time: 46.7 us -> 47.3 us (1.013)
  Pallas kernels: 42.7 us -> 43.2 us
    pallas_call x1, Pallas kernels: 42.7 us -> 43.2 us  [body(): pl.pallas_call(functools.partial(kernel, chips), out_shape=jax.ShapeDtype...]
where the time goes in v5:
time: 47.3 us; the launch traced here: 47 us
  Pallas kernels  43.2 us (91%)
  local copies, waits for them, and re-layouts  3.76 us (8%)
    pallas_call x1, Pallas kernels, body(): pl.pallas_call(functools.partial(kernel, chips), out_shape=jax.ShapeDtype...  43.2 us
    transpose x1, local copies, waits for them, and re-layouts, body(): jnp.transpose(up_weight, (1, 2, 0, 3)).reshape(TAPS, slice_out, channels)  1.99 us
    unnamed x1, local copies, waits for them, and re-layouts  1.77 us

profile of v5, /device:TPU:1, one launch (start us, length us, event | category | flops | bytes accessed | tf_op | source)
XLA Modules:
  0.0 47.0 jit_solution(16523875235184296594)
XLA Ops:
  0.0 2.0 %copy.8 = bf16[2,2,64,1024]{3,2,1,0:T(8,128)(2,1)} copy(bf16[2,2,64,1024]{3,1,0,2:T(2,128)(2,1)} %bitcast.10) | data formatting | bytes 1048576 | tf_op jit(solution)/shard_map/transpose | solution.py:385
  2.0 43.2 %shard_map.73 = bf16[4,96,512]{2,1,0:T(8,128)(2,1)} custom-call(bf16[2,48,1024]{2,1,0:T(8,128)(2,1)} %coarse.1, bf16[1152,1024]{1,0:T(8,128)(2,1)} %bitcast.8, bf16[4,64,1024]{2,1,0:T(8,128)(2,1)} %bitcast.9, f32[1,128]{1,0:T(1,128)} %bitcast.11, f32[1,128]{1,0:T(1,128)} %bitcast.12, f32[1,128]{1,0:T(1,128)} %bitcast.13, bf16[64]{0:T(256)(128)(2,1)} %up_bias.1), custom_call_target="tpu_custom_call" | custom-call | tf_op jit(solution)/shard_map/pallas_call | solution.py:389
  45.2 1.8 %copy.10 = bf16[4,96,512]{2,1,0:T(8,128)(2,1)} copy(bf16[4,96,512]{2,1,0:T(8,128)(2,1)} %shard_map.73) | data formatting | bytes 786432

commit v6 on v4

--- a/solution.py
+++ b/solution.py
@@ -138,20 +138,20 @@
         )
     pl.semaphore_wait(barrier, devices - 1 + TAPS - 1)
 
-    for h in range(rows):
-        for direction in range(2):
-
-            @pl.when(onward(direction)[1])
-            def _():
-                coarse_line(direction, z, h, coarse.at[h]).start()
-
-        coarse_sib(z, h, coarse.at[h]).start()
     for direction in range(2):
 
         @pl.when(onward(direction)[1])
         def _():
             up_line(direction, z, up_w.at[part]).start()
 
+    for h in range(rows):
+        for direction in range(2):
+
+            @pl.when(onward(direction)[1])
+            def _():
+                coarse_line(direction, z, h, coarse.at[h]).start()
+
+        coarse_sib(z, h, coarse.at[h]).start()
     up_sib(z, up_w).start()
 
     lanes = lax.broadcasted_iota(jnp.int32, (slice_out, decoded), 1)
@@ -258,7 +258,7 @@
                     coarse_wait(2 * src + 1 - core, h)
                 conv_pair(src)
 
-        @pl.when(k > 1)
+        @pl.when(jnp.logical_and(k > 1, k < chips - 1))
         def _():
             spread(k - 1)
 
@@ -295,6 +295,9 @@
 
     lax.fori_loop(1, devices, send_act, 0)
     act_all[me] = act[me]
+
+    if chips > 2:
+        spread(chips - 2)
 
     def early(i, carry):
         other = lax.rem(me + i, devices)

time: 46.7 us -> 46.4 us (level)
  no operation moved by 1% of the time
where the time goes in v6:
time: 46.4 us; the launch traced here: 46.1 us
  Pallas kernels  42.4 us (91%)
  local copies, waits for them, and re-layouts  3.76 us (8%)
    pallas_call x1, Pallas kernels, body(): pl.pallas_call(functools.partial(kernel, chips), out_shape=jax.ShapeDtype...  42.4 us
    transpose x1, local copies, waits for them, and re-layouts, body(): jnp.transpose(up_weight, (1, 2, 0, 3)).reshape(TAPS, slice_out, channels)  1.99 us
    unnamed x1, local copies, waits for them, and re-layouts  1.77 us

profile of v6, /device:TPU:1, one launch (start us, length us, event | category | flops | bytes accessed | tf_op | source)
XLA Modules:
  0.0 46.1 jit_solution(6681292913086183292)
XLA Ops:
  0.0 2.0 %copy.8 = bf16[2,2,64,1024]{3,2,1,0:T(8,128)(2,1)} copy(bf16[2,2,64,1024]{3,1,0,2:T(2,128)(2,1)} %bitcast.10) | data formatting | bytes 1048576 | tf_op jit(solution)/shard_map/transpose | solution.py:379
  2.0 42.4 %shard_map.73 = bf16[4,96,512]{2,1,0:T(8,128)(2,1)} custom-call(bf16[2,48,1024]{2,1,0:T(8,128)(2,1)} %coarse.1, bf16[1152,1024]{1,0:T(8,128)(2,1)} %bitcast.8, bf16[4,64,1024]{2,1,0:T(8,128)(2,1)} %bitcast.9, f32[1,128]{1,0:T(1,128)} %bitcast.11, f32[1,128]{1,0:T(1,128)} %bitcast.12, f32[1,128]{1,0:T(1,128)} %bitcast.13, bf16[64]{0:T(256)(128)(2,1)} %up_bias.1), custom_call_target="tpu_custom_call" | custom-call | tf_op jit(solution)/shard_map/pallas_call | solution.py:383
  44.4 1.8 %copy.10 = bf16[4,96,512]{2,1,0:T(8,128)(2,1)} copy(bf16[4,96,512]{2,1,0:T(8,128)(2,1)} %shard_map.73) | data formatting | bytes 786432
